TPU v7x, 32 devices: a whole 2x2x4 slice. The times are simulated.
32 devices in a mesh: rows: 8 (over z, y), feat: 4 (over x, core).
Axes of the slice: x: 2, y: 2, z: 4, core: 2. Of those that a mesh axis runs over, the one named last changes fastest.
Arguments:
- feats: bfloat16 [256, 16384], P('feat', 'rows'), may hold values from -6 to 6
- weight: bfloat16 [256, 256], P('feat'), may hold values from -0.375 to 0.375
- bias: float32 [256], P('feat'), may hold values from -3 to 3
- tile_cols: int32 [1024], P('rows'), may hold values from 0 to 127, as said below
- tile_values: bfloat16 [1024, 128, 128], P('rows'), may hold values from -0.1875 to 0.1875
- cotangent: bfloat16 [256, 16384], P('feat', 'rows'), may hold values from -6 to 6
Outputs:
- hidden_out: bfloat16 [256, 16384], P('feat', 'rows')
- grad_input: float32 [256, 16384], P('feat', 'rows')
- grad_weight: float32 [256, 256], P('feat')
- grad_bias: float32 [256], P('feat')
Inputs may be any that keep to these rules, and one draw needn't show every extreme that they name: `tile_cols`: column blocks of tiles. In each row block the first 4 tiles have column blocks on the same index of rows as the row block (index = column block // 16). Of the other tiles of one index of rows, at most 16 have column blocks on any one index, and in every draw one index receives exactly 16 such tiles from every index.
All inputs are finite; a program needn't handle non-finite values.
Results may differ from a plain program's by a relative error of at most 0.0058.
Values may be sent and summed in bfloat16 or wider, within the bound.
A program may use at most 128 MiB of HBM per device.

v0:
```python
import math

import jax
import jax.numpy as jnp
from jax import lax
from jax.sharding import PartitionSpec as P

TL = 4


def local(feats, weight, bias, tile_cols, tile_values, cotangent):
    hid_dev = weight.shape[1] // lax.axis_size("feat")
    nodes_dev = feats.shape[1]
    block = tile_values.shape[1]
    row_blocks = nodes_dev // block
    peers = lax.axis_size("rows")
    tiles_dev = tile_cols.shape[0]
    per_block = tiles_dev // row_blocks
    remote_count = row_blocks * (per_block - TL)
    capacity = 2 * remote_count // peers
    num_slots = peers * capacity
    columns = weight
    mixed = lax.psum_scatter(
        lax.dot_general(
            columns, feats, (((0,), (0,)), ((), ())), preferred_element_type=jnp.float32
        ),
        "feat",
        scatter_dimension=0,
        tiled=True,
    )
    proj = mixed.astype(jnp.bfloat16)
    grid = tile_cols.reshape(row_blocks, per_block)
    tiles = tile_values.reshape(row_blocks, per_block, block, block)
    local_tiles = tiles[:, :TL]
    remote_tiles = tiles[:, TL:]
    local_cols = grid[:, :TL] % row_blocks
    remote_cols = grid[:, TL:].reshape(-1)
    remote_owner = remote_cols // row_blocks
    remote_local = remote_cols % row_blocks
    owner_onehot = (remote_owner[:, None] == jnp.arange(peers)[None, :]).astype(jnp.int32)
    before = jnp.cumsum(owner_onehot, axis=0) - owner_onehot
    ranks = jnp.sum(before * owner_onehot, axis=1)
    slots = remote_owner * capacity + ranks
    request = jnp.full((num_slots,), -1, jnp.int32).at[slots].set(remote_local)
    slot_tile = (
        jnp.full((num_slots,), -1, jnp.int32)
        .at[slots]
        .set(jnp.arange(remote_count, dtype=jnp.int32))
    )
    wanted = lax.all_to_all(
        request.reshape(peers, capacity), "rows", split_axis=0, concat_axis=0, tiled=True
    ).reshape(-1)
    gathered = lax.all_gather(proj, "rows", axis=1, tiled=True)
    gathered = gathered.reshape(hid_dev, -1, block)
    fetched = jnp.take(gathered, tile_cols, axis=1).reshape(hid_dev, row_blocks, per_block, block)
    local_part = jnp.einsum(
        "fbtk,btnk->bfn", fetched[:, :, :TL], local_tiles, preferred_element_type=jnp.float32
    )
    remote_part = jnp.einsum(
        "fbtk,btnk->bfn", fetched[:, :, TL:], remote_tiles, preferred_element_type=jnp.float32
    )
    summed = local_part + remote_part
    pre = summed.transpose(1, 0, 2).reshape(hid_dev, nodes_dev) + bias[:, None]
    hidden_out = jax.nn.silu(pre).astype(jnp.bfloat16)
    sigma = jax.nn.sigmoid(pre)
    grad_pre = cotangent.astype(jnp.float32) * (sigma * (1.0 + pre * (1.0 - sigma)))
    bias_part = jnp.sum(grad_pre, axis=1)
    grad_blocks = (
        grad_pre.astype(jnp.bfloat16).reshape(hid_dev, row_blocks, block).transpose(1, 0, 2)
    )
    local_back = jnp.einsum(
        "bfn,btnk->btfk", grad_blocks, local_tiles, preferred_element_type=jnp.float32
    )
    local_onehot = (local_cols[:, :, None] == jnp.arange(row_blocks)[None, None, :]).astype(
        jnp.float32
    )
    grad_proj_blocks = jnp.einsum(
        "bts,btfk->sfk", local_onehot, local_back, precision=lax.Precision.HIGHEST
    )
    remote_back = jnp.einsum(
        "bfn,btnk->btfk", grad_blocks, remote_tiles, preferred_element_type=jnp.float32
    )
    remote_back = remote_back.reshape(remote_count, hid_dev, block)
    filled = (slot_tile >= 0).astype(jnp.float32)
    outgoing_back = remote_back[jnp.maximum(slot_tile, 0)] * filled[:, None, None]
    outgoing_back = outgoing_back.reshape(peers, capacity, hid_dev, block)
    returned = lax.all_to_all(
        outgoing_back, "rows", split_axis=0, concat_axis=0, tiled=True
    ).reshape(num_slots, hid_dev, block)
    wanted_onehot = (wanted[:, None] == jnp.arange(row_blocks)[None, :]).astype(jnp.float32)
    grad_proj_blocks = grad_proj_blocks + jnp.einsum(
        "sb,sfk->bfk", wanted_onehot, returned, precision=lax.Precision.HIGHEST
    )
    grad_proj = grad_proj_blocks.transpose(1, 0, 2).reshape(hid_dev, nodes_dev).astype(jnp.bfloat16)
    piece = lax.all_gather(grad_proj, "feat", axis=0, tiled=True)
    columns = weight
    input_grad = jnp.dot(columns, piece, preferred_element_type=jnp.float32)
    partial_rows = lax.dot_general(
        feats, piece, (((1,), (1,)), ((), ())), preferred_element_type=jnp.float32
    )
    weight_total, bias_total = lax.psum((partial_rows, bias_part), "rows")
    divisor = math.sqrt(nodes_dev * peers)
    return (hidden_out, input_grad, weight_total / divisor, bias_total / divisor)


def solution(mesh):
    placed = (
        P("feat", "rows"),
        P("feat", None),
        P("feat"),
        P("rows"),
        P("rows", None, None),
        P("feat", "rows"),
    )
    return jax.shard_map(
        local,
        mesh=mesh,
        in_specs=placed,
        out_specs=(P("feat", "rows"), P("feat", "rows"), P("feat", None), P("feat")),
        check_vma=False,
    )
```

profile of v0, /device:TPU:0, one launch (start us, length us, event | category | flops | bytes accessed | tf_op | source)
XLA Modules:
  0.0 316.2 jit_solution(8668631288506056465)
XLA Ops:
  7.2 0.0 copy-start
  7.2 0.0 reduce-scatter.2.cloned.1.call-start
  7.2 0.9 copy-done
  8.1 2.6 fusion.50
  10.7 0.0 copy-start.6
  10.7 0.0 reduce-scatter.2.cloned.1.call-update
  10.7 0.0 all-gather.3.cloned.1.call-start
  10.8 34.2 %reduce-scatter.2.cloned.1.call-done = f32[64,2048]{1,0:T(8,128)} async-done(((f32[256,2048]{1,0:T(8,128)}), f32[64,2048]{1,0:T(8,128)}) %reduce-scatter.2.cloned.1.call-update) | async-done | bytes 524304 | tf_op jit(solution)/shard_map/reduce_scatter | solution.py:23
  45.0 1.8 convert_element_type.27
  46.8 0.0 all-gather.3.cloned.1.call-update
  46.8 0.0 copy-done.6
  46.8 0.1 reshape.160
  46.9 0.1 fusion.49
  47.0 0.1 reshape.163
  47.1 0.1 reshape.162
  47.2 0.1 fusion.33
  47.2 0.1 reduce_window_sum.11
  47.3 0.2 select_reduce_fusion
  47.5 0.8 scatter_custom_fusion
  48.3 0.7 all_to_all.9
  49.0 5.5 %all-to-all-start = ((s32[8,1,16]{2,1,0:T(1,128)}), s32[8,1,16]{2,1,0:T(1,128)S(1)}, u32[]{:S(2)}, u32[]{:S(2)}) async-start(s32[8,1,16]{2,1,0:T(1,128)} %bitcast.17), calls=%async_computation.1 | async-start | bytes 8192 | tf_op jit(solution)/shard_map/all_to_all | solution.py:50
  54.5 0.1 broadcast_in_dim.26
  54.6 0.8 scatter_custom_fusion.1
  55.4 0.1 reshape.166
  55.5 41.8 %all-gather.3.cloned.1.call-done = bf16[64,16384]{1,0:T(8,128)(2,1)} async-done(((bf16[64,2048]{1,0:T(8,128)(2,1)}), bf16[64,16384]{1,0:T(8,128)(2,1)}) %all-gather.3.cloned.1.call-update) | async-done | bytes 2097168 | tf_op jit(solution)/shard_map/all_gather | solution.py:53
  97.3 2.2 copy_bitcast_fusion
  99.5 2.2 gather_fusion
  101.6 0.0 copy-start.1
  101.6 0.0 copy-start.2
  101.6 2.9 fusion.16
  104.6 0.2 copy-done.1
  104.8 0.7 copy-done.2
  105.5 0.0 copy-start.3
  105.5 0.9 fusion.25
  106.3 0.1 copy-done.3
  106.4 0.0 copy-done.5
  106.4 1.1 fusion.48
  107.5 0.4 fusion.2
  108.0 2.8 gather_fusion.1
  110.7 2.5 broadcast_multiply_fusion
  113.3 4.3 %copy.32 = f32[8,16,64,128]{3,1,2,0:T(8,128)} copy(f32[8,16,64,128]{3,2,1,0:T(8,128)S(1)} %broadcast_multiply_fusion) | data formatting | bytes 8388608 | tf_op jit(solution)/shard_map/mul | solution.py:85
  117.6 0.0 all-to-all-done
  117.6 4.5 %all-to-all-start.1 = ((f32[8,16,64,128]{3,1,2,0:T(8,128)}), f32[8,16,64,128]{3,1,2,0:T(8,128)}, u32[]{:S(2)}, u32[]{:S(2)}) async-start(f32[8,16,64,128]{3,1,2,0:T(8,128)} %copy.32), calls=%async_computation.2 | async-start | bytes 8388608 | tf_op jit(solution)/shard_map/all_to_all | solution.py:87
  122.2 0.2 all-gather.5.cloned.1.call-start
  122.4 0.1 copy.28
  122.5 0.5 broadcast.163
  123.0 0.7 reduce.3
  123.7 0.1 eq.51
  123.7 2.0 fusion.10
  125.8 2.3 fusion.13
  128.1 86.5 %all-to-all-done.1 = f32[8,16,64,128]{3,1,2,0:T(8,128)} async-done(((f32[8,16,64,128]{3,1,2,0:T(8,128)}), f32[8,16,64,128]{3,1,2,0:T(8,128)}, u32[]{:S(2)}, u32[]{:S(2)}) %all-to-all-start.1) | async-done | bytes 4194336 | tf_op jit(solution)/shard_map/all_to_all | solution.py:87
  214.5 2.8 copy.33
  217.3 1.5 fusion.28
  218.8 0.8 copy.62
  219.6 0.0 all-gather.5.cloned.1.call-update
  219.6 0.0 all-reduce.2.cloned.1.call-start
  219.7 19.5 %psum.15 = f32[64]{0:T(128)S(1)} all-reduce(f32[64]{0:T(128)S(1)} %get-tuple-element.4), channel_id=1, replica_groups=mesh['rows'=8,'feat'=4] {'rows'}, use_global_device_ids=true, to_apply=%region_7.8 | all-reduce | flops 64 | bytes 512 | tf_op jit(solution)/shard_map/psum | solution.py:101
  239.1 0.5 broadcast_multiply_fusion.2
  239.6 2.3 convolution_bitcast_fusion.1
  241.9 0.0 all-reduce.2.cloned.1.call-update
  242.0 0.0 copy-done.4
  242.0 2.3 convolution_bitcast_fusion
  244.3 63.9 %all-reduce.2.cloned.1.call-done = f32[64,256]{1,0:T(8,128)} async-done(((f32[64,256]{1,0:T(8,128)}), f32[64,256]{1,0:T(8,128)}) %all-reduce.2.cloned.1.call-update) | async-done | bytes 65552 | tf_op jit(solution)/shard_map/psum | solution.py:101
  308.2 1.5 broadcast_multiply_fusion.1
  (12 shorter events, 0.1 us)
Async XLA Ops:
  7.2 1.0 copy-start
  7.2 37.8 %reduce-scatter.2.cloned.1.call-start = ((), (), s32[]{:S(2)}) async-start(), calls=%async_computation.3 | async-start | bytes 2621440 | tf_op jit(solution)/shard_map/reduce_scatter | solution.py:23
  10.7 36.1 %copy-start.6 = (s32[128]{0:T(128)S(1)}, s32[128]{0:T(128)}, u32[]{:S(2)}) copy-start(s32[128]{0:T(128)} %param.9) | copy-start | bytes 1540
  10.7 86.6 %all-gather.3.cloned.1.call-start = ((), (), s32[]{:S(2)}) async-start(), calls=%async_computation.4 | async-start | bytes 2359296 | tf_op jit(solution)/shard_map/all_gather | solution.py:53
  49.0 68.6 %all-to-all-start = ((s32[8,1,16]{2,1,0:T(1,128)}), s32[8,1,16]{2,1,0:T(1,128)S(1)}, u32[]{:S(2)}, u32[]{:S(2)}) async-start(s32[8,1,16]{2,1,0:T(1,128)} %bitcast.17), calls=%async_computation.1 | async-start | bytes 8192 | tf_op jit(solution)/shard_map/all_to_all | solution.py:50
  101.6 3.1 copy-start.1
  101.6 3.8 %copy-start.2 = (bf16[128,64,128]{2,1,0:T(8,128)(2,1)S(1)}, bf16[128,64,128]{2,1,0:T(8,128)(2,1)}, u32[]{:S(2)}) copy-start(bf16[128,64,128]{2,1,0:T(8,128)(2,1)} %gather_fusion) | copy-start | bytes 6291460
  105.5 0.9 copy-start.3
  105.5 1.0 copy-start.5
  117.6 96.9 %all-to-all-start.1 = ((f32[8,16,64,128]{3,1,2,0:T(8,128)}), f32[8,16,64,128]{3,1,2,0:T(8,128)}, u32[]{:S(2)}, u32[]{:S(2)}) async-start(f32[8,16,64,128]{3,1,2,0:T(8,128)} %copy.32), calls=%async_computation.2 | async-start | bytes 8388608 | tf_op jit(solution)/shard_map/all_to_all | solution.py:87
  122.2 117.5 %all-gather.5.cloned.1.call-start = ((), (), s32[]{:S(2)}) async-start(), calls=%async_computation.5 | async-start | bytes 1310720 | tf_op jit(solution)/shard_map/all_gather | solution.py:95
  218.8 23.2 %copy-start.4 = (bf16[64,256]{1,0:T(8,128)(2,1)S(1)}, bf16[64,256]{1,0:T(8,128)(2,1)}, u32[]{:S(2)}) copy-start(bf16[64,256]{1,0:T(8,128)(2,1)} %param.7) | copy-start | bytes 98308
  219.6 88.6 %all-reduce.2.cloned.1.call-start = ((), (), s32[]{:S(2)}) async-start(), calls=%async_computation.6 | async-start | bytes 131072 | tf_op jit(solution)/shard_map/psum | solution.py:101
Sparse Core Ops, SparseCore 0:
  10.8 34.1 reduce-scatter.1
  48.0 49.2 all-gather.2
  219.7 15.7 all-gather.4
  242.1 66.0 all-reduce.1
where the time goes:
time: 317 us; the launch traced here: 316 us
  waiting for transfers between devices  226 us (71%)
  local copies, waits for them, and re-layouts  20.2 us (6%)
  blocking collectives  19.5 us (6%)
  matrix products  17.3 us (5%)
  between operations  14 us (4%)
  starting transfers between devices  10.4 us (3%)
  other arithmetic  8.57 us (3%)
    all_to_all x1, waiting for transfers between devices, local(): lax.all_to_all(outgoing_back, 'rows', split_axis=0, concat_axis=0, tiled=...  86.5 us
    psum x1, waiting for transfers between devices, local(): weight_total, bias_total = lax.psum((partial_rows, bias_part), 'rows')  63.9 us
    all_gather x1, waiting for transfers between devices, local(): gathered = lax.all_gather(proj, 'rows', axis=1, tiled=True)  41.8 us
    reduce_scatter x1, waiting for transfers between devices, local(): lax.psum_scatter(lax.dot_general(columns, feats, (((0,), (0,)), ((), ()))...  34.2 us
    psum x1, blocking collectives, local(): weight_total, bias_total = lax.psum((partial_rows, bias_part), 'rows')  19.5 us
  transfers between devices with their start and end apart: 6, of which 4 were waited for; matrix products, arithmetic and copies ran while one was open for 10% of the time, Pallas kernels for 0%

commit v1 on v0

v1 whole, which is shorter than its diff:
```python
import functools
import math

import jax
import jax.numpy as jnp
from jax import lax
from jax.experimental import pallas as pl
from jax.experimental.pallas import tpu as pltpu
from jax.sharding import PartitionSpec as P

MESH = pl.DeviceIdType.MESH
F32 = jnp.float32
BF16 = jnp.bfloat16


def kernel(
    n,
    chunks,
    sum_inside,
    scale,
    cols,
    order,
    order_row,
    keep,
    last,
    has,
    feats,
    weight,
    bias,
    tiles_hbm,
    cot_hbm,
    hidden,
    grad_in,
    grad_w,
    grad_b,
    gbuf,
    tiles,
    cot,
    zall,
    gall,
    ubuf,
    sbuf,
    back,
    wall,
    wt,
    bias_acc,
    wsum,
    wland,
    wpiece,
    local_sem,
    w_send,
    w_recv,
    ag_send,
    ag_recv,
    fe_send,
    fe_recv,
    rs_send,
    rs_recv,
    s1_send,
    s1_recv,
    s2_send,
    s2_recv,
):
    width, nodes = feats.shape
    block = tiles.shape[1]
    row_blocks = nodes // block
    per_block = tiles.shape[0] // row_blocks
    in_chunk = row_blocks // chunks
    cw = in_chunk * block
    half = n // 2
    row = lax.axis_index("rows")
    fe = lax.axis_index("feat")
    odd = lax.rem(row, 2)
    pos = (1 - odd) * (row // 2) + odd * (n - 1 - row // 2)

    def row_at(p):
        p = lax.rem(p + 2 * n, n)
        far = p // half
        return (1 - far) * (2 * p) + far * (2 * n - 1 - 2 * p)

    near = (row_at(pos + 1), row_at(pos - 1))
    sib = fe + 1 - 2 * lax.rem(fe, 2)
    opp = lax.rem(fe + 2, 4)
    opp_sib = lax.rem(sib + 2, 4)

    tile_copy = pltpu.make_async_copy(tiles_hbm, tiles, local_sem.at[0])
    cot_copy = pltpu.make_async_copy(cot_hbm, cot, local_sem.at[1])
    tile_copy.start()
    cot_copy.start()

    barrier = pltpu.get_barrier_semaphore()
    if sum_inside:
        others = [lax.rem(row + k, n) for k in range(1, n)]
    else:
        others = list(near)
    for peer in others:
        pl.semaphore_signal(barrier, inc=1, device_id={"rows": peer}, device_id_type=MESH)
    for peer in (sib, opp, opp_sib):
        pl.semaphore_signal(barrier, inc=1, device_id={"feat": peer}, device_id_type=MESH)

    for b in range(row_blocks):
        gbuf[row * row_blocks + b] = feats[:, b * block : (b + 1) * block]
    wall[pl.ds(pl.multiple_of(fe * width, width), width), :] = weight[...]
    pl.semaphore_wait(barrier, len(others) + 3)

    def span(owner, c):
        return gbuf.at[pl.ds(owner * row_blocks + c * in_chunk, in_chunk)]

    def gather_copy(way, d, c):
        sign = 1 - 2 * way
        at = span(row_at(pos - sign * d), c)
        return pltpu.make_async_remote_copy(
            src_ref=at,
            dst_ref=at,
            send_sem=ag_send.at[way, d, c],
            recv_sem=ag_recv.at[way, d, c],
            device_id={"rows": near[way]},
            device_id_type=MESH,
        )

    def gather_arrival(way, d, c):
        sign = 1 - 2 * way
        at = span(row_at(pos - sign * (d + 1)), c)
        return pltpu.make_async_remote_copy(
            src_ref=at,
            dst_ref=at,
            send_sem=ag_send.at[way, d, c],
            recv_sem=ag_recv.at[way, d, c],
            device_id={"rows": near[way]},
            device_id_type=MESH,
        )

    def moves(way, d):
        if d < half - 1:
            return list(range(chunks))
        if way == 0:
            return list(range(chunks // 2))
        return list(range(chunks // 2, chunks))

    def weight_copy(k, peer):
        at = wall.at[pl.ds(pl.multiple_of(fe * width, width), width), :]
        return pltpu.make_async_remote_copy(
            src_ref=at,
            dst_ref=at,
            send_sem=w_send.at[k],
            recv_sem=w_recv.at[k],
            device_id={"feat": peer},
            device_id_type=MESH,
        )

    def weight_arrival(k, peer):
        at = wall.at[pl.ds(pl.multiple_of(peer * width, width), width), :]
        return pltpu.make_async_remote_copy(
            src_ref=at,
            dst_ref=at,
            send_sem=w_send.at[k],
            recv_sem=w_recv.at[k],
            device_id={"feat": peer},
            device_id_type=MESH,
        )

    for c in range(chunks):
        for way in range(2):
            if c in moves(way, 0):
                gather_copy(way, 0, c).start()
    for k, peer in enumerate((sib, opp, opp_sib)):
        weight_copy(k, peer).start()
    for d in range(1, half):
        for c in range(chunks):
            for way in range(2):
                if c in moves(way, d - 1):
                    gather_arrival(way, d - 1, c).wait_recv()
                if c in moves(way, d):
                    gather_copy(way, d, c).start()
        if d == 1:
            for k, peer in enumerate((sib, opp, opp_sib)):
                weight_arrival(k, peer).wait_recv()
            wt[...] = wall[...].astype(F32).T.astype(BF16)
            tile_copy.wait()
            cot_copy.wait()
    for way in range(2):
        for c in moves(way, half - 1):
            gather_arrival(way, half - 1, c).wait_recv()

    def feat_move(buf, kind, hop, c, owner, peer):
        at = buf.at[c, pl.ds(pl.multiple_of(owner * width, width), width), :]
        return pltpu.make_async_remote_copy(
            src_ref=at,
            dst_ref=at,
            send_sem=fe_send.at[kind, hop, c],
            recv_sem=fe_recv.at[kind, hop, c],
            device_id={"feat": peer},
            device_id_type=MESH,
        )

    def feat_start(buf, kind, c):
        feat_move(buf, kind, 0, c, fe, opp).start()
        feat_move(buf, kind, 1, c, fe, sib).start()

    def feat_pass(buf, kind, c):
        feat_move(buf, kind, 0, c, opp, opp).wait_recv()
        feat_move(buf, kind, 2, c, opp, sib).start()

    def feat_arrive(buf, kind, c):
        feat_move(buf, kind, 1, c, sib, sib).wait_recv()
        feat_move(buf, kind, 2, c, opp_sib, sib).wait_recv()

    mine = pl.ds(pl.multiple_of(fe * width, width), width)

    for c in range(chunks):

        def one_row(r, carry, c=c):
            total = jnp.zeros((width, block), F32)
            for t in range(per_block):
                i = (c * in_chunk + r) * per_block + t
                total += lax.dot_general(
                    gbuf[cols[i]], tiles[i], (((1,), (1,)), ((), ())), preferred_element_type=F32
                )
            zall[c, mine, pl.ds(pl.multiple_of(r * block, block), block)] = total.astype(BF16)
            return carry

        lax.fori_loop(0, in_chunk, one_row, 0)
        feat_start(zall, 0, c)
        if c > 0:
            feat_pass(zall, 0, c - 1)
    feat_pass(zall, 0, chunks - 1)

    w_cols = wt[mine, :]
    for c in range(chunks):
        feat_arrive(zall, 0, c)
        pre = jnp.dot(w_cols, zall[c], preferred_element_type=F32) + bias[...]
        sigma = jax.nn.sigmoid(pre)
        hidden[:, c * cw : (c + 1) * cw] = (pre * sigma).astype(BF16)
        g = cot[:, c * cw : (c + 1) * cw].astype(F32) * (sigma * (1.0 + pre * (1.0 - sigma)))
        gall[c, mine, :] = g.astype(BF16)
        feat_start(gall, 1, c)
        folded = g[:, :block]
        for b in range(1, in_chunk):
            folded = folded + g[:, b * block : (b + 1) * block]
        bias_acc[...] = folded if c == 0 else bias_acc[...] + folded
        if c > 0:
            feat_pass(gall, 1, c - 1)
    feat_pass(gall, 1, chunks - 1)

    w_sum = jnp.zeros((width, wall.shape[1]), F32)
    for c in range(chunks):
        feat_arrive(gall, 1, c)
        u = jnp.dot(weight[...], gall[c], preferred_element_type=F32).astype(BF16)
        for b in range(in_chunk):
            ubuf[c * in_chunk + b] = u[:, b * block : (b + 1) * block]
        w_sum += lax.dot_general(
            zall[c, mine, :], gall[c], (((1,), (1,)), ((), ())), preferred_element_type=F32
        )
    hid = wall.shape[1]
    wsum[:, :hid] = w_sum
    wsum[:, hid:] = jnp.broadcast_to(jnp.sum(bias_acc[...], axis=1, keepdims=True), bias_acc.shape)

    piece = width // n if sum_inside else width

    def piece_at(ref, owner):
        return ref.at[pl.ds(pl.multiple_of(owner * piece, piece), piece), :]

    def piece_copy(k):
        to = lax.rem(row + k, n)
        return pltpu.make_async_remote_copy(
            src_ref=piece_at(wsum, to),
            dst_ref=wland.at[k],
            send_sem=s1_send.at[k],
            recv_sem=s1_recv.at[k],
            device_id={"rows": to},
            device_id_type=MESH,
        )

    def total_copy(k):
        to = lax.rem(row + k, n)
        return pltpu.make_async_remote_copy(
            src_ref=piece_at(wpiece, row),
            dst_ref=piece_at(wpiece, row),
            send_sem=s2_send.at[k],
            recv_sem=s2_recv.at[k],
            device_id={"rows": to},
            device_id_type=MESH,
        )

    def total_arrival(k):
        owner = lax.rem(row + n - k, n)
        return pltpu.make_async_remote_copy(
            src_ref=piece_at(wpiece, owner),
            dst_ref=piece_at(wpiece, owner),
            send_sem=s2_send.at[k],
            recv_sem=s2_recv.at[k],
            device_id={"rows": owner},
            device_id_type=MESH,
        )

    if sum_inside:
        for k in range(1, n):
            piece_copy(k).start()

    group = 8

    def some_terms(i, running):
        for j in range(group):
            at = i * group + j
            sbuf[at] = jnp.dot(
                ubuf[order_row[at]], tiles[order[at]], preferred_element_type=F32
            )
        for j in range(group):
            at = i * group + j
            running = sbuf[at] + keep[at] * running
            sbuf[at] = running
        return running

    lax.fori_loop(0, tiles.shape[0] // group, some_terms, jnp.zeros((width, block), F32))

    for way in range(2):
        for d in range(half):
            for c in moves(way, d):
                gather_copy(way, d, c).wait_send()

    def own_term(at):
        return sbuf[last[at]] * has[at]

    def back_copy(way, d, c):
        sign = 1 - 2 * way
        return pltpu.make_async_remote_copy(
            src_ref=span(row_at(pos + sign * d), c),
            dst_ref=back.at[way, d - 1, pl.ds(c * in_chunk, in_chunk)],
            send_sem=rs_send.at[way, d - 1, c],
            recv_sem=rs_recv.at[way, d - 1, c],
            device_id={"rows": near[way]},
            device_id_type=MESH,
        )

    for d in range(half, 0, -1):
        for c in range(chunks):
            for way in range(2):
                if c not in moves(way, d - 1):
                    continue
                joined = d < half and c in moves(way, d)
                if joined:
                    back_copy(way, d + 1, c).wait_recv()
                sign = 1 - 2 * way
                owner = row_at(pos + sign * d)
                for b in range(c * in_chunk, (c + 1) * in_chunk):
                    at = owner * row_blocks + b
                    value = own_term(at)
                    if joined:
                        value = value + back[way, d, b].astype(F32)
                    gbuf[at] = value.astype(BF16)
                back_copy(way, d, c).start()
        if sum_inside and d == half - 1:
            whole = wsum[pl.ds(pl.multiple_of(row * piece, piece), piece), :]
            for k in range(1, n):
                piece_copy(k).wait_recv()
                whole = whole + wland[k]
            wpiece[pl.ds(pl.multiple_of(row * piece, piece), piece), :] = whole * scale
            for k in range(1, n):
                total_copy(k).start()

    for c in range(chunks):
        for way in range(2):
            back_copy(way, 1, c).wait_recv()
        for b in range(c * in_chunk, (c + 1) * in_chunk):
            value = own_term(row * row_blocks + b)
            value = value + back[0, 0, b].astype(F32) + back[1, 0, b].astype(F32)
            grad_in[:, b * block : (b + 1) * block] = value

    if sum_inside:
        for k in range(1, n):
            total_arrival(k).wait_recv()
        grad_w[...] = wpiece[:, :hid]
        grad_b[...] = wpiece[:, hid:]
    else:
        grad_w[...] = wsum[:, :hid]
        grad_b[...] = wsum[:, hid:]

    for k, peer in enumerate((sib, opp, opp_sib)):
        weight_copy(k, peer).wait_send()
    for kind, buf in enumerate((zall, gall)):
        for c in range(chunks):
            feat_move(buf, kind, 0, c, fe, opp).wait_send()
            feat_move(buf, kind, 1, c, fe, sib).wait_send()
            feat_move(buf, kind, 2, c, opp, sib).wait_send()
    for way in range(2):
        for d in range(1, half + 1):
            for c in moves(way, d - 1):
                back_copy(way, d, c).wait_send()
    if sum_inside:
        for k in range(1, n):
            piece_copy(k).wait_send()
            total_copy(k).wait_send()


def local(feats, weight, bias, tile_cols, tile_values, cotangent):
    width, nodes = feats.shape
    hid = weight.shape[1]
    count, block = tile_values.shape[0], tile_values.shape[1]
    n = lax.axis_size("rows")
    row_blocks = nodes // block
    per_block = count // row_blocks
    chunks = 4 if n <= 8 else 2
    half = n // 2
    sum_inside = n == 8
    scale = 1.0 / math.sqrt(nodes * n)

    index = jnp.arange(count, dtype=jnp.int32)
    earlier = (tile_cols[None, :] < tile_cols[:, None]) | (
        (tile_cols[None, :] == tile_cols[:, None]) & (index[None, :] < index[:, None])
    )
    rank = jnp.sum(earlier.astype(jnp.int32), axis=1)
    placed = rank[None, :] == index[:, None]
    order = jnp.sum(jnp.where(placed, index[None, :], 0), axis=1)
    order_row = order // per_block
    in_order = jnp.sum(jnp.where(placed, tile_cols[None, :], 0), axis=1)
    keep = jnp.concatenate([jnp.zeros((1,), F32), (in_order[1:] == in_order[:-1]).astype(F32)])
    dest = jnp.arange(n * row_blocks, dtype=jnp.int32)
    upto = jnp.sum((tile_cols[None, :] <= dest[:, None]).astype(jnp.int32), axis=1)
    below = jnp.sum((tile_cols[None, :] < dest[:, None]).astype(jnp.int32), axis=1)
    has = (upto > below).astype(F32)
    last = jnp.maximum(upto - 1, 0)

    smem = pl.BlockSpec(memory_space=pltpu.SMEM)
    vmem = pl.BlockSpec(memory_space=pltpu.VMEM)
    anywhere = pl.BlockSpec(memory_space=pl.ANY)
    dma = pltpu.SemaphoreType.DMA
    piece = width // n if sum_inside else 8
    hidden, grad_in, grad_w, grad_b = pl.pallas_call(
        functools.partial(kernel, n, chunks, sum_inside, scale),
        out_shape=(
            jax.ShapeDtypeStruct((width, nodes), BF16),
            jax.ShapeDtypeStruct((width, nodes), F32),
            jax.ShapeDtypeStruct((width, hid), F32),
            jax.ShapeDtypeStruct((width, block), F32),
        ),
        in_specs=[smem] * 6 + [vmem] * 3 + [anywhere] * 2,
        out_specs=(vmem,) * 4,
        scratch_shapes=[
            pltpu.VMEM((n * row_blocks, width, block), BF16),
            pltpu.VMEM((count, block, block), BF16),
            pltpu.VMEM((width, nodes), BF16),
            pltpu.VMEM((chunks, 4 * width, nodes // chunks), BF16),
            pltpu.VMEM((chunks, 4 * width, nodes // chunks), BF16),
            pltpu.VMEM((row_blocks, width, block), BF16),
            pltpu.VMEM((count, width, block), F32),
            pltpu.VMEM((2, half, row_blocks, width, block), BF16),
            pltpu.VMEM((4 * width, hid), BF16),
            pltpu.VMEM((hid, 4 * width), BF16),
            pltpu.VMEM((width, block), F32),
            pltpu.VMEM((width, hid + block), F32),
            pltpu.VMEM((n if sum_inside else 1, piece, hid + block), F32),
            pltpu.VMEM((width, hid + block), F32),
            dma((2,)),
            dma((3,)),
            dma((3,)),
            dma((2, half, chunks)),
            dma((2, half, chunks)),
            dma((2, 3, chunks)),
            dma((2, 3, chunks)),
            dma((2, half, chunks)),
            dma((2, half, chunks)),
            dma((n,)),
            dma((n,)),
            dma((n,)),
            dma((n,)),
        ],
        compiler_params=pltpu.CompilerParams(
            collective_id=0, has_side_effects=True, vmem_limit_bytes=52 * 1024 * 1024
        ),
        cost_estimate=pl.CostEstimate(
            flops=2 * 2 * count * width * block * block + 6 * width * hid * nodes,
            bytes_accessed=2 * count * block * block,
            transcendentals=width * nodes,
        ),
    )(
        tile_cols,
        order,
        order_row,
        keep,
        last,
        has,
        feats,
        weight,
        bias[:, None],
        tile_values,
        cotangent,
    )
    bias_total = grad_b[:, 0]
    if not sum_inside:
        grad_w, bias_total = lax.psum((grad_w * scale, bias_total * scale), "rows")
    return hidden, grad_in, grad_w, bias_total


def solution(mesh):
    placed = (
        P("feat", "rows"),
        P("feat", None),
        P("feat"),
        P("rows"),
        P("rows", None, None),
        P("feat", "rows"),
    )
    return jax.shard_map(
        local,
        mesh=mesh,
        in_specs=placed,
        out_specs=(P("feat", "rows"), P("feat", "rows"), P("feat", None), P("feat")),
        check_vma=False,
    )
```

time: 317 us -> 89.1 us (0.28)
  waiting for transfers between devices: 226 us -> 0 us
  Pallas kernels: 0 us -> 79.5 us
  blocking collectives: 19.5 us -> 0 us
  matrix products: 17.3 us -> 0 us
  local copies, waits for them, and re-layouts: 20.2 us -> 6.81 us
  between operations: 14 us -> 0.66 us
  starting transfers between devices: 10.4 us -> 0 us
  other arithmetic: 8.57 us -> 1.87 us
    all_to_all x2 -> x0, waiting for transfers between devices: 86.5 us -> none  [the longest x1 86.5 us: local(): lax.all_to_all(outgoing_back, 'rows', split_axis=0, concat_axis=0, tiled=...]
    pallas_call x0 -> x1, Pallas kernels: none -> 79.5 us  [local(): pl.pallas_call(functools.partial(kernel, n, chunks, sum_inside, scale), o...]
    psum x1 -> x0, waiting for transfers between devices: 63.9 us -> none  [local(): weight_total, bias_total = lax.psum((partial_rows, bias_part), 'rows')]
    all_gather x2 -> x0, waiting for transfers between devices: 41.8 us -> none  [the longest x1 41.8 us: local(): gathered = lax.all_gather(proj, 'rows', axis=1, tiled=True)]
    reduce_scatter x1 -> x0, waiting for transfers between devices: 34.2 us -> none  [local(): lax.psum_scatter(lax.dot_general(columns, feats, (((0,), (0,)), ((), ()))...]
    psum x1 -> x0, blocking collectives: 19.5 us -> none  [local(): weight_total, bias_total = lax.psum((partial_rows, bias_part), 'rows')]
    dot_general x9 -> x0, matrix products: 17.3 us -> none  [the longest x1 2.93 us: local(): jnp.einsum('fbtk,btnk->bfn', fetched[:, :, :TL], local_tiles, preferred_e...]
    all_to_all x2 -> x0, starting transfers between devices: 10 us -> none  [the longest x1 5.51 us: local(): lax.all_to_all(request.reshape(peers, capacity), 'rows', split_axis=0, co...]
  transfers between devices with their start and end apart: 6 -> 0, of which waited for: 4 -> 0; matrix products, arithmetic and copies ran while one was open for 10% -> 0% of each run, Pallas kernels for 0% -> 0%
where the time goes in v1:
time: 89.1 us; the launch traced here: 88.8 us
  Pallas kernels  79.5 us (89%)
  local copies, waits for them, and re-layouts  6.81 us (8%)
  other arithmetic  1.87 us (2%)
    pallas_call x1, Pallas kernels, local(): pl.pallas_call(functools.partial(kernel, n, chunks, sum_inside, scale), o...  79.5 us
    unnamed x11, local copies, waits for them, and re-layouts  5.43 us

profile of v1, /device:TPU:0, one launch (start us, length us, event | category | flops | bytes accessed | tf_op | source)
XLA Modules:
  0.0 88.8 jit_solution(13934246815369387005)
XLA Ops:
  0.6 0.9 %convert_reduce_fusion.2 = s32[128]{0:T(128)S(1)} fusion(s32[128]{0:T(128)} %cols.1), kind=kLoop, calls=%fused_computation.7 | loop fusion | flops 114560 | bytes 1024 | tf_op jit(solution)/shard_map/reduce_sum | solution.py:411
  1.5 0.8 convert_reduce_fusion
  2.3 0.1 slice_compare_fusion
  2.4 0.1 add_convert_fusion
  2.5 0.7 copy.12.bias
  3.3 0.0 copy-start
  3.3 0.9 %copy-done = bf16[64,2048]{1,0:T(8,128)(2,1)S(1)} copy-done((bf16[64,2048]{1,0:T(8,128)(2,1)S(1)}, bf16[64,2048]{1,0:T(8,128)(2,1)}, u32[]{:S(2)}) %copy-start) | copy-done | bytes 262168
  4.2 0.0 copy-start.1
  4.2 0.9 %copy-done.1 = bf16[64,2048]{1,0:T(8,128)(2,1)S(1)} copy-done((bf16[64,2048]{1,0:T(8,128)(2,1)S(1)}, bf16[64,2048]{1,0:T(8,128)(2,1)}, u32[]{:S(2)}) %copy-start.1) | copy-done | bytes 262168
  5.2 0.0 copy-start.2
  5.2 0.8 copy-done.2
  5.9 0.0 copy-start.3
  5.9 0.7 copy-done.3
  6.6 79.5 %shard_map.93 = (bf16[64,2048]{1,0:T(8,128)(2,1)S(1)}, f32[64,2048]{1,0:T(8,128)S(1)}, f32[64,256]{1,0:T(8,128)S(1)}, f32[64,128]{1,0:T(8,128)S(1)}) custom-call(s32[128]{0:T(128)S(1)} %copy-done.3, s32[128]{0:T(128)S(1)} %get-tuple-element.14.order, s32[128]{0:T(128)S(1)} %get-tuple-element.16.order_row, f32[128]{0:T(128)S(1)} %get-tuple-element.18.keep, ...), custom_call_target="tpu_custom_call" | custom-call | flops 738197504 | bytes 4194304 | tf_op jit(solution)/shard_map/pallas_call | solution.py:428
  86.1 0.6 slice_reduce_fusion
  86.7 0.7 copy.16
  87.4 0.8 copy.17
  88.2 0.6 copy.18
  (1 shorter events, 0.0 us)
Async XLA Ops:
  3.3 0.9 %copy-start = (bf16[64,2048]{1,0:T(8,128)(2,1)S(1)}, bf16[64,2048]{1,0:T(8,128)(2,1)}, u32[]{:S(2)}) copy-start(bf16[64,2048]{1,0:T(8,128)(2,1)} %feats.1) | copy-start | bytes 786436
  4.2 0.9 %copy-start.1 = (bf16[64,2048]{1,0:T(8,128)(2,1)S(1)}, bf16[64,2048]{1,0:T(8,128)(2,1)}, u32[]{:S(2)}) copy-start(bf16[64,2048]{1,0:T(8,128)(2,1)} %cot_hbm.1) | copy-start | bytes 786436
  5.2 0.8 copy-start.2
  5.9 0.7 copy-start.3

commit v2 on v1

--- a/solution.py
+++ b/solution.py
@@ -9,6 +9,7 @@
 from jax.sharding import PartitionSpec as P
 
 MESH = pl.DeviceIdType.MESH
+TL = 4
 F32 = jnp.float32
 BF16 = jnp.bfloat16
 
@@ -20,26 +21,30 @@
     scale,
     cols,
     order,
-    order_row,
     keep,
     last,
     has,
+    bias,
     feats,
     weight,
-    bias,
     tiles_hbm,
     cot_hbm,
-    hidden,
-    grad_in,
-    grad_w,
+    hidden_hbm,
+    grad_in_hbm,
+    grad_w_hbm,
     grad_b,
+    own,
     gbuf,
     tiles,
     cot,
     zall,
     gall,
     ubuf,
+    tbuf,
     sbuf,
+    zloc,
+    hidden,
+    grad_in,
     back,
     wall,
     wt,
@@ -48,6 +53,8 @@
     wland,
     wpiece,
     local_sem,
+    feats_sem,
+    out_sem,
     w_send,
     w_recv,
     ag_send,
@@ -85,8 +92,19 @@
 
     tile_copy = pltpu.make_async_copy(tiles_hbm, tiles, local_sem.at[0])
     cot_copy = pltpu.make_async_copy(cot_hbm, cot, local_sem.at[1])
-    tile_copy.start()
-    cot_copy.start()
+    feats_copies = [
+        pltpu.make_async_copy(
+            feats.at[:, pl.ds(b * block, block)],
+            own.at[b],
+            feats_sem.at[b],
+        )
+        for b in range(row_blocks)
+    ]
+    for copy in feats_copies:
+        copy.start()
+    mine = pl.ds(pl.multiple_of(fe * width, width), width)
+    weight_in = pltpu.make_async_copy(weight, wall.at[mine, :], local_sem.at[2])
+    weight_in.start()
 
     barrier = pltpu.get_barrier_semaphore()
     if sum_inside:
@@ -98,9 +116,11 @@
     for peer in (sib, opp, opp_sib):
         pl.semaphore_signal(barrier, inc=1, device_id={"feat": peer}, device_id_type=MESH)
 
-    for b in range(row_blocks):
-        gbuf[row * row_blocks + b] = feats[:, b * block : (b + 1) * block]
-    wall[pl.ds(pl.multiple_of(fe * width, width), width), :] = weight[...]
+    for copy in feats_copies:
+        copy.wait()
+    tile_copy.start()
+    cot_copy.start()
+    weight_in.wait()
     pl.semaphore_wait(barrier, len(others) + 3)
 
     def span(owner, c):
@@ -109,8 +129,9 @@
     def gather_copy(way, d, c):
         sign = 1 - 2 * way
         at = span(row_at(pos - sign * d), c)
-        return pltpu.make_async_remote_copy(
-            src_ref=at,
+        src = own.at[pl.ds(c * in_chunk, in_chunk)] if d == 0 else at
+        return pltpu.make_async_remote_copy(
+            src_ref=src,
             dst_ref=at,
             send_sem=ag_send.at[way, d, c],
             recv_sem=ag_recv.at[way, d, c],
@@ -165,6 +186,17 @@
                 gather_copy(way, 0, c).start()
     for k, peer in enumerate((sib, opp, opp_sib)):
         weight_copy(k, peer).start()
+    def products(get, r, first, count):
+        left = jnp.concatenate([get(r * per_block + first + t) for t in range(count)], axis=1)
+        right = jnp.concatenate([tiles[r * per_block + first + t] for t in range(count)], axis=1)
+        return lax.dot_general(left, right, (((1,), (1,)), ((), ())), preferred_element_type=F32)
+
+    def local_products(r):
+        zloc[r] = products(lambda i: own[cols[i]], r, 0, TL)
+
+    for b in range(row_blocks):
+        gbuf[row * row_blocks + b] = own[b]
+    done = 0
     for d in range(1, half):
         for c in range(chunks):
             for way in range(2):
@@ -172,12 +204,19 @@
                     gather_arrival(way, d - 1, c).wait_recv()
                 if c in moves(way, d):
                     gather_copy(way, d, c).start()
+            if d == 1 and c == 0:
+                tile_copy.wait()
+            if done < row_blocks:
+                for r in range(done, min(done + 2, row_blocks)):
+                    local_products(r)
+                done = min(done + 2, row_blocks)
         if d == 1:
             for k, peer in enumerate((sib, opp, opp_sib)):
                 weight_arrival(k, peer).wait_recv()
             wt[...] = wall[...].astype(F32).T.astype(BF16)
-            tile_copy.wait()
             cot_copy.wait()
+    for r in range(done, row_blocks):
+        local_products(r)
     for way in range(2):
         for c in moves(way, half - 1):
             gather_arrival(way, half - 1, c).wait_recv()
@@ -205,17 +244,11 @@
         feat_move(buf, kind, 1, c, sib, sib).wait_recv()
         feat_move(buf, kind, 2, c, opp_sib, sib).wait_recv()
 
-    mine = pl.ds(pl.multiple_of(fe * width, width), width)
-
     for c in range(chunks):
 
         def one_row(r, carry, c=c):
-            total = jnp.zeros((width, block), F32)
-            for t in range(per_block):
-                i = (c * in_chunk + r) * per_block + t
-                total += lax.dot_general(
-                    gbuf[cols[i]], tiles[i], (((1,), (1,)), ((), ())), preferred_element_type=F32
-                )
+            at = c * in_chunk + r
+            total = zloc[at] + products(lambda i: gbuf[cols[i]], at, TL, per_block - TL)
             zall[c, mine, pl.ds(pl.multiple_of(r * block, block), block)] = total.astype(BF16)
             return carry
 
@@ -226,9 +259,15 @@
     feat_pass(zall, 0, chunks - 1)
 
     w_cols = wt[mine, :]
+    w_rows = wall[mine, :]
+    diagonal = lax.broadcasted_iota(jnp.int32, (width, width), 0) == lax.broadcasted_iota(
+        jnp.int32, (width, width), 1
+    )
+    bias_row = jnp.broadcast_to(bias[...], (width, width))
+    bias_col = jnp.sum(jnp.where(diagonal, bias_row, 0.0), axis=1, keepdims=True)
     for c in range(chunks):
         feat_arrive(zall, 0, c)
-        pre = jnp.dot(w_cols, zall[c], preferred_element_type=F32) + bias[...]
+        pre = jnp.dot(w_cols, zall[c], preferred_element_type=F32) + bias_col
         sigma = jax.nn.sigmoid(pre)
         hidden[:, c * cw : (c + 1) * cw] = (pre * sigma).astype(BF16)
         g = cot[:, c * cw : (c + 1) * cw].astype(F32) * (sigma * (1.0 + pre * (1.0 - sigma)))
@@ -241,13 +280,22 @@
         if c > 0:
             feat_pass(gall, 1, c - 1)
     feat_pass(gall, 1, chunks - 1)
+    hidden_out = pltpu.make_async_copy(hidden, hidden_hbm, out_sem.at[0])
+    hidden_out.start()
+
+    def terms(r, first, count):
+        right = jnp.concatenate([tiles[r * per_block + first + t] for t in range(count)], axis=1)
+        out = jnp.dot(ubuf[r], right, preferred_element_type=F32)
+        for t in range(count):
+            tbuf[r * per_block + first + t] = out[:, t * block : (t + 1) * block]
 
     w_sum = jnp.zeros((width, wall.shape[1]), F32)
     for c in range(chunks):
         feat_arrive(gall, 1, c)
-        u = jnp.dot(weight[...], gall[c], preferred_element_type=F32).astype(BF16)
+        u = jnp.dot(w_rows, gall[c], preferred_element_type=F32).astype(BF16)
         for b in range(in_chunk):
             ubuf[c * in_chunk + b] = u[:, b * block : (b + 1) * block]
+            terms(c * in_chunk + b, TL, per_block - TL)
         w_sum += lax.dot_general(
             zall[c, mine, :], gall[c], (((1,), (1,)), ((), ())), preferred_element_type=F32
         )
@@ -298,20 +346,20 @@
             piece_copy(k).start()
 
     group = 8
-
-    def some_terms(i, running):
-        for j in range(group):
-            at = i * group + j
-            sbuf[at] = jnp.dot(
-                ubuf[order_row[at]], tiles[order[at]], preferred_element_type=F32
-            )
-        for j in range(group):
-            at = i * group + j
-            running = sbuf[at] + keep[at] * running
-            sbuf[at] = running
-        return running
-
-    lax.fori_loop(0, tiles.shape[0] // group, some_terms, jnp.zeros((width, block), F32))
+    locals_count = row_blocks * TL
+    remote_count = tiles.shape[0] - locals_count
+
+    def running_sums(first, count):
+        def some_sums(i, running):
+            for j in range(group):
+                at = first + i * group + j
+                running = tbuf[order[at]] + keep[at] * running
+                sbuf[at] = running
+            return running
+
+        lax.fori_loop(0, count // group, some_sums, jnp.zeros((width, block), F32))
+
+    running_sums(0, remote_count)
 
     for way in range(2):
         for d in range(half):
@@ -332,23 +380,34 @@
             device_id_type=MESH,
         )
 
+    def send_back(way, d, c):
+        joined = d < half and c in moves(way, d)
+        if joined:
+            back_copy(way, d + 1, c).wait_recv()
+        sign = 1 - 2 * way
+        owner = row_at(pos + sign * d)
+        for b in range(c * in_chunk, (c + 1) * in_chunk):
+            at = owner * row_blocks + b
+            value = own_term(at)
+            if joined:
+                value = value + back[way, d, b].astype(F32)
+            gbuf[at] = value.astype(BF16)
+        back_copy(way, d, c).start()
+
+    orders = (
+        list(range(chunks // 2, chunks)) + list(range(chunks // 2)),
+        list(range(chunks)),
+    )
+    done = 0
     for d in range(half, 0, -1):
-        for c in range(chunks):
+        for k in range(chunks):
             for way in range(2):
-                if c not in moves(way, d - 1):
-                    continue
-                joined = d < half and c in moves(way, d)
-                if joined:
-                    back_copy(way, d + 1, c).wait_recv()
-                sign = 1 - 2 * way
-                owner = row_at(pos + sign * d)
-                for b in range(c * in_chunk, (c + 1) * in_chunk):
-                    at = owner * row_blocks + b
-                    value = own_term(at)
-                    if joined:
-                        value = value + back[way, d, b].astype(F32)
-                    gbuf[at] = value.astype(BF16)
-                back_copy(way, d, c).start()
+                if orders[way][k] in moves(way, d - 1):
+                    send_back(way, d, orders[way][k])
+            if d < half or half == 1:
+                for r in range(done, min(done + 2, row_blocks)):
+                    terms(r, 0, TL)
+                done = min(done + 2, row_blocks)
         if sum_inside and d == half - 1:
             whole = wsum[pl.ds(pl.multiple_of(row * piece, piece), piece), :]
             for k in range(1, n):
@@ -357,23 +416,38 @@
             wpiece[pl.ds(pl.multiple_of(row * piece, piece), piece), :] = whole * scale
             for k in range(1, n):
                 total_copy(k).start()
+    for r in range(done, row_blocks):
+        terms(r, 0, TL)
+    running_sums(remote_count, locals_count)
+    for b in range(row_blocks):
+        at = n * row_blocks + b
+        grad_in[:, b * block : (b + 1) * block] = own_term(row * row_blocks + b) + own_term(at)
+
+    def grad_in_copy(c):
+        at = pl.ds(c * cw, cw)
+        return pltpu.make_async_copy(grad_in.at[:, at], grad_in_hbm.at[:, at], out_sem.at[2 + c])
 
     for c in range(chunks):
         for way in range(2):
             back_copy(way, 1, c).wait_recv()
         for b in range(c * in_chunk, (c + 1) * in_chunk):
-            value = own_term(row * row_blocks + b)
+            value = grad_in[:, b * block : (b + 1) * block]
             value = value + back[0, 0, b].astype(F32) + back[1, 0, b].astype(F32)
             grad_in[:, b * block : (b + 1) * block] = value
+        grad_in_copy(c).start()
 
     if sum_inside:
         for k in range(1, n):
             total_arrival(k).wait_recv()
-        grad_w[...] = wpiece[:, :hid]
-        grad_b[...] = wpiece[:, hid:]
-    else:
-        grad_w[...] = wsum[:, :hid]
-        grad_b[...] = wsum[:, hid:]
+    result = wpiece if sum_inside else wsum
+    grad_w_out = pltpu.make_async_copy(result.at[:, pl.ds(0, hid)], grad_w_hbm, out_sem.at[1])
+    grad_w_out.start()
+    bias_cols = jnp.broadcast_to(result[:, hid : hid + 1], (width, width))
+    grad_b[...] = jnp.sum(jnp.where(diagonal, bias_cols, 0.0), axis=0, keepdims=True)
+    hidden_out.wait()
+    grad_w_out.wait()
+    for c in range(chunks):
+        grad_in_copy(c).wait()
 
     for k, peer in enumerate((sib, opp, opp_sib)):
         weight_copy(k, peer).wait_send()
@@ -405,18 +479,21 @@
     scale = 1.0 / math.sqrt(nodes * n)
 
     index = jnp.arange(count, dtype=jnp.int32)
-    earlier = (tile_cols[None, :] < tile_cols[:, None]) | (
-        (tile_cols[None, :] == tile_cols[:, None]) & (index[None, :] < index[:, None])
+    is_local = index % per_block < TL
+    cols = jnp.where(is_local, tile_cols % row_blocks, tile_cols)
+    key = tile_cols + jnp.where(is_local, n * row_blocks, 0)
+    earlier = (key[None, :] < key[:, None]) | (
+        (key[None, :] == key[:, None]) & (index[None, :] < index[:, None])
     )
     rank = jnp.sum(earlier.astype(jnp.int32), axis=1)
     placed = rank[None, :] == index[:, None]
     order = jnp.sum(jnp.where(placed, index[None, :], 0), axis=1)
-    order_row = order // per_block
-    in_order = jnp.sum(jnp.where(placed, tile_cols[None, :], 0), axis=1)
+    in_order = jnp.sum(jnp.where(placed, key[None, :], 0), axis=1)
     keep = jnp.concatenate([jnp.zeros((1,), F32), (in_order[1:] == in_order[:-1]).astype(F32)])
-    dest = jnp.arange(n * row_blocks, dtype=jnp.int32)
-    upto = jnp.sum((tile_cols[None, :] <= dest[:, None]).astype(jnp.int32), axis=1)
-    below = jnp.sum((tile_cols[None, :] < dest[:, None]).astype(jnp.int32), axis=1)
+    dest = jnp.arange((n + 1) * row_blocks, dtype=jnp.int32)
+    dest = jnp.where(dest < n * row_blocks, dest, dest + lax.axis_index("rows") * row_blocks)
+    upto = jnp.sum((key[None, :] <= dest[:, None]).astype(jnp.int32), axis=1)
+    below = jnp.sum((key[None, :] < dest[:, None]).astype(jnp.int32), axis=1)
     has = (upto > below).astype(F32)
     last = jnp.maximum(upto - 1, 0)
 
@@ -431,11 +508,12 @@
             jax.ShapeDtypeStruct((width, nodes), BF16),
             jax.ShapeDtypeStruct((width, nodes), F32),
             jax.ShapeDtypeStruct((width, hid), F32),
-            jax.ShapeDtypeStruct((width, block), F32),
+            jax.ShapeDtypeStruct((1, width), F32),
         ),
-        in_specs=[smem] * 6 + [vmem] * 3 + [anywhere] * 2,
-        out_specs=(vmem,) * 4,
+        in_specs=[smem] * 5 + [vmem] + [anywhere] * 4,
+        out_specs=(anywhere, anywhere, anywhere, vmem),
         scratch_shapes=[
+            pltpu.VMEM((row_blocks, width, block), BF16),
             pltpu.VMEM((n * row_blocks, width, block), BF16),
             pltpu.VMEM((count, block, block), BF16),
             pltpu.VMEM((width, nodes), BF16),
@@ -443,6 +521,10 @@
             pltpu.VMEM((chunks, 4 * width, nodes // chunks), BF16),
             pltpu.VMEM((row_blocks, width, block), BF16),
             pltpu.VMEM((count, width, block), F32),
+            pltpu.VMEM((count, width, block), F32),
+            pltpu.VMEM((row_blocks, width, block), F32),
+            pltpu.VMEM((width, nodes), BF16),
+            pltpu.VMEM((width, nodes), F32),
             pltpu.VMEM((2, half, row_blocks, width, block), BF16),
             pltpu.VMEM((4 * width, hid), BF16),
             pltpu.VMEM((hid, 4 * width), BF16),
@@ -450,7 +532,9 @@
             pltpu.VMEM((width, hid + block), F32),
             pltpu.VMEM((n if sum_inside else 1, piece, hid + block), F32),
             pltpu.VMEM((width, hid + block), F32),
-            dma((2,)),
+            dma((3,)),
+            dma((row_blocks,)),
+            dma((2 + chunks,)),
             dma((3,)),
             dma((3,)),
             dma((2, half, chunks)),
@@ -473,19 +557,18 @@
             transcendentals=width * nodes,
         ),
     )(
-        tile_cols,
+        cols,
         order,
-        order_row,
-        keep,
+            keep,
         last,
         has,
+        bias[None, :],
         feats,
         weight,
-        bias[:, None],
         tile_values,
         cotangent,
     )
-    bias_total = grad_b[:, 0]
+    bias_total = grad_b[0]
     if not sum_inside:
         grad_w, bias_total = lax.psum((grad_w * scale, bias_total * scale), "rows")
     return hidden, grad_in, grad_w, bias_total

time: 89.1 us -> 84.2 us (0.945)
  Pallas kernels: 79.5 us -> 76 us
    pallas_call x1, Pallas kernels: 79.5 us -> 76 us  [local(): pl.pallas_call(functools.partial(kernel, n, chunks, sum_inside, scale), o...]
    unnamed x11 -> x12, local copies, waits for them, and re-layouts: 5.43 us -> 5.94 us
where the time goes in v2:
time: 84.2 us; the launch traced here: 84 us
  Pallas kernels  76 us (90%)
  local copies, waits for them, and re-layouts  5.94 us (7%)
  other arithmetic  1.36 us (2%)
    pallas_call x1, Pallas kernels, local(): pl.pallas_call(functools.partial(kernel, n, chunks, sum_inside, scale), o...  76 us
    unnamed x12, local copies, waits for them, and re-layouts  5.94 us

profile of v2, /device:TPU:0, one launch (start us, length us, event | category | flops | bytes accessed | tf_op | source)
XLA Modules:
  0.0 84.0 jit_solution(1445812586448461145)
XLA Ops:
  0.6 0.7 fusion.2
  1.3 0.2 convert_reduce_fusion.2
  1.5 0.1 select_reduce_fusion
  1.6 0.1 slice_compare_fusion
  1.7 0.1 add_convert_fusion.keep
  1.8 0.2 convert_reduce_fusion
  2.0 0.0 copy-start
  2.0 0.9 %copy-done = bf16[64,2048]{1,0:T(8,128)(2,1)S(1)} copy-done((bf16[64,2048]{1,0:T(8,128)(2,1)S(1)}, bf16[64,2048]{1,0:T(8,128)(2,1)}, u32[]{:S(2)}) %copy-start) | copy-done | bytes 262168
  3.0 0.0 copy-start.1
  3.0 0.9 %copy-done.1 = bf16[64,2048]{1,0:T(8,128)(2,1)S(1)} copy-done((bf16[64,2048]{1,0:T(8,128)(2,1)S(1)}, bf16[64,2048]{1,0:T(8,128)(2,1)}, u32[]{:S(2)}) %copy-start.1) | copy-done | bytes 262168
  3.9 0.0 copy-start.2
  3.9 0.8 copy-done.2
  4.7 0.0 copy-start.3
  4.7 0.7 copy-done.3
  5.3 76.0 %shard_map.93 = (bf16[64,2048]{1,0:T(8,128)(2,1)S(1)}, f32[64,2048]{1,0:T(8,128)S(1)}, f32[64,256]{1,0:T(8,128)S(1)}, f32[1,64]{1,0:T(1,128)S(1)}) custom-call(s32[128]{0:T(128)S(1)} %get-tuple-element.17.cols, s32[128]{0:T(128)S(1)} %get-tuple-element.15.order, f32[128]{0:T(128)S(1)} %add_convert_fusion.keep, s32[144]{0:T(256)S(1)} %add_maximum_fusion.last, ...), custom_call_target="tpu_custom_call" | custom-call | flops 738197504 | bytes 4194304 | tf_op jit(solution)/shard_map/pallas_call | solution.py:505
  81.3 0.7 copy.14
  82.0 0.8 copy.15
  82.8 0.6 copy.16
  83.5 0.5 copy.17
  (3 shorter events, 0.0 us)
Async XLA Ops:
  2.0 1.0 %copy-start = (bf16[64,2048]{1,0:T(8,128)(2,1)S(1)}, bf16[64,2048]{1,0:T(8,128)(2,1)}, u32[]{:S(2)}) copy-start(bf16[64,2048]{1,0:T(8,128)(2,1)} %feats.1) | copy-start | bytes 786436
  3.0 0.9 %copy-start.1 = (bf16[64,2048]{1,0:T(8,128)(2,1)S(1)}, bf16[64,2048]{1,0:T(8,128)(2,1)}, u32[]{:S(2)}) copy-start(bf16[64,2048]{1,0:T(8,128)(2,1)} %cot_hbm.1) | copy-start | bytes 786436
  3.9 0.8 copy-start.2
  4.7 0.7 copy-start.3

commit v3 on v2

--- a/solution.py
+++ b/solution.py
@@ -466,6 +466,15 @@
             total_copy(k).wait_send()
 
 
+def hand_over(*refs):
+    sems = refs[8]
+    copies = [pltpu.make_async_copy(refs[k], refs[4 + k], sems.at[k]) for k in range(4)]
+    for copy in copies:
+        copy.start()
+    for copy in copies:
+        copy.wait()
+
+
 def local(feats, weight, bias, tile_cols, tile_values, cotangent):
     width, nodes = feats.shape
     hid = weight.shape[1]
@@ -549,7 +558,7 @@
             dma((n,)),
         ],
         compiler_params=pltpu.CompilerParams(
-            collective_id=0, has_side_effects=True, vmem_limit_bytes=52 * 1024 * 1024
+            collective_id=0, has_side_effects=True, vmem_limit_bytes=63 * 1024 * 1024
         ),
         cost_estimate=pl.CostEstimate(
             flops=2 * 2 * count * width * block * block + 6 * width * hid * nodes,
@@ -568,10 +577,18 @@
         tile_values,
         cotangent,
     )
-    bias_total = grad_b[0]
     if not sum_inside:
-        grad_w, bias_total = lax.psum((grad_w * scale, bias_total * scale), "rows")
-    return hidden, grad_in, grad_w, bias_total
+        grad_w, grad_b = lax.psum((grad_w * scale, grad_b * scale), "rows")
+    results = (hidden, grad_in, grad_w, grad_b)
+    hidden, grad_in, grad_w, grad_b = pl.pallas_call(
+        hand_over,
+        out_shape=tuple(jax.ShapeDtypeStruct(a.shape, a.dtype) for a in results),
+        in_specs=[anywhere] * 4,
+        out_specs=(anywhere,) * 4,
+        scratch_shapes=[dma((4,))],
+        compiler_params=pltpu.CompilerParams(vmem_limit_bytes=63 * 1024 * 1024),
+    )(*results)
+    return hidden, grad_in, grad_w, grad_b[0]
 
 
 def solution(mesh):

time: 84.2 us -> 109 us (1.29)
  Pallas kernels: 76 us -> 104 us
  local copies, waits for them, and re-layouts: 5.94 us -> 0 us
  other arithmetic: 1.36 us -> 4.04 us
    pallas_call x0 -> x1, Pallas kernels: none -> 27 us  [local(): pl.pallas_call(hand_over, out_shape=tuple((jax.ShapeDtypeStruct(a.shape,...]
    unnamed x12 -> x0, local copies, waits for them, and re-layouts: 5.94 us -> none
    pallas_call x1, Pallas kernels: 76 us -> 77.2 us  [local(): pl.pallas_call(functools.partial(kernel, n, chunks, sum_inside, scale), o...]
where the time goes in v3:
time: 109 us
  Pallas kernels  104 us (95%)
  other arithmetic  4.04 us (4%)
    pallas_call x1, Pallas kernels, local(): pl.pallas_call(functools.partial(kernel, n, chunks, sum_inside, scale), o...  77.2 us
    pallas_call x1, Pallas kernels, local(): pl.pallas_call(hand_over, out_shape=tuple((jax.ShapeDtypeStruct(a.shape,...  27 us

profile of v3, /device:TPU:0, one launch (start us, length us, event | category | flops | bytes accessed | tf_op | source)
XLA Modules:
  0.0 108.8 jit_solution(12121466582570183306)
XLA Ops:
  0.6 1.2 %fusion.2 = (s32[128]{0:T(128)S(1)}, s32[128]{0:T(128)}) fusion(s32[128]{0:T(128)} %param.9), kind=kLoop, calls=%fused_computation.19 | loop fusion | flops 2688 | bytes 1536 | tf_op jit(solution)/shard_map/add | solution.py:493
  1.8 0.2 convert_reduce_fusion.2
  2.0 0.6 select_reduce_fusion
  2.6 0.1 slice_compare_fusion
  2.7 0.6 add_convert_fusion.keep
  3.3 0.2 convert_reduce_fusion
  3.5 0.6 compare_convert_fusion.has
  4.1 0.6 add_maximum_fusion.last
  4.7 77.2 %shard_map.93 = (bf16[64,2048]{1,0:T(8,128)(2,1)}, f32[64,2048]{1,0:T(8,128)}, f32[64,256]{1,0:T(8,128)}, f32[1,64]{1,0:T(1,128)}) custom-call(s32[128]{0:T(128)} %get-tuple-element.25.cols, s32[128]{0:T(128)} %get-tuple-element.23.order, f32[128]{0:T(128)} %add_convert_fusion.keep, s32[144]{0:T(256)} %add_maximum_fusion.last, f32[144]{0:T(256)} %compare_convert_fusion.has, ...), custom_call_target="tpu_custom_call" | custom-call | flops 738197504 | bytes 4194304 | tf_op jit(solution)/shard_map/pallas_call | solution.py:514
  81.9 27.0 %shard_map.94 = (bf16[64,2048]{1,0:T(8,128)(2,1)}, f32[64,2048]{1,0:T(8,128)}, f32[64,256]{1,0:T(8,128)}, f32[1,64]{1,0:T(1,128)}) custom-call(bf16[64,2048]{1,0:T(8,128)(2,1)} %get-tuple-element.12.refs_0_, f32[64,2048]{1,0:T(8,128)} %get-tuple-element.13.refs_1_, f32[64,256]{1,0:T(8,128)} %get-tuple-element.14.refs_2_, f32[1,64]{1,0:T(1,128)} %get-tuple-element.15.refs_3_), custom_call_target="tpu_custom_call" | custom-call | tf_op jit(solution)/shard_map/pallas_call | solution.py:583
  (1 shorter events, 0.0 us)

commit v4 on v2

--- a/solution.py
+++ b/solution.py
@@ -37,7 +37,7 @@
     gbuf,
     tiles,
     cot,
-    zall,
+    fall,
     gall,
     ubuf,
     tbuf,
@@ -92,17 +92,15 @@
 
     tile_copy = pltpu.make_async_copy(tiles_hbm, tiles, local_sem.at[0])
     cot_copy = pltpu.make_async_copy(cot_hbm, cot, local_sem.at[1])
+    mine = pl.ds(pl.multiple_of(fe * width, width), width)
     feats_copies = [
         pltpu.make_async_copy(
-            feats.at[:, pl.ds(b * block, block)],
-            own.at[b],
-            feats_sem.at[b],
-        )
-        for b in range(row_blocks)
+            feats.at[:, pl.ds(c * cw, cw)], fall.at[c, mine, :], feats_sem.at[c]
+        )
+        for c in range(chunks)
     ]
     for copy in feats_copies:
         copy.start()
-    mine = pl.ds(pl.multiple_of(fe * width, width), width)
     weight_in = pltpu.make_async_copy(weight, wall.at[mine, :], local_sem.at[2])
     weight_in.start()
 
@@ -180,12 +178,51 @@
             device_id_type=MESH,
         )
 
+    def feat_move(buf, kind, hop, c, owner, peer):
+        at = buf.at[c, pl.ds(pl.multiple_of(owner * width, width), width), :]
+        return pltpu.make_async_remote_copy(
+            src_ref=at,
+            dst_ref=at,
+            send_sem=fe_send.at[kind, hop, c],
+            recv_sem=fe_recv.at[kind, hop, c],
+            device_id={"feat": peer},
+            device_id_type=MESH,
+        )
+
+    def feat_start(buf, kind, c):
+        feat_move(buf, kind, 0, c, fe, opp).start()
+        feat_move(buf, kind, 1, c, fe, sib).start()
+
+    def feat_pass(buf, kind, c):
+        feat_move(buf, kind, 0, c, opp, opp).wait_recv()
+        feat_move(buf, kind, 2, c, opp, sib).start()
+
+    def feat_arrive(buf, kind, c):
+        feat_move(buf, kind, 1, c, sib, sib).wait_recv()
+        feat_move(buf, kind, 2, c, opp_sib, sib).wait_recv()
+
+    peers = (sib, opp, opp_sib)
+    for k, peer in enumerate(peers):
+        weight_copy(k, peer).start()
     for c in range(chunks):
+        feat_start(fall, 0, c)
+    for k, peer in enumerate(peers):
+        weight_arrival(k, peer).wait_recv()
+    wt[...] = wall[...].astype(F32).T.astype(BF16)
+    w_cols = wt[mine, :]
+    w_rows = wall[mine, :]
+    feat_pass(fall, 0, 0)
+    for c in range(chunks):
+        if c + 1 < chunks:
+            feat_pass(fall, 0, c + 1)
+        feat_arrive(fall, 0, c)
+        proj = jnp.dot(w_cols, fall[c], preferred_element_type=F32).astype(BF16)
+        for b in range(in_chunk):
+            own[c * in_chunk + b] = proj[:, b * block : (b + 1) * block]
         for way in range(2):
             if c in moves(way, 0):
                 gather_copy(way, 0, c).start()
-    for k, peer in enumerate((sib, opp, opp_sib)):
-        weight_copy(k, peer).start()
+
     def products(get, r, first, count):
         left = jnp.concatenate([get(r * per_block + first + t) for t in range(count)], axis=1)
         right = jnp.concatenate([tiles[r * per_block + first + t] for t in range(count)], axis=1)
@@ -211,9 +248,6 @@
                     local_products(r)
                 done = min(done + 2, row_blocks)
         if d == 1:
-            for k, peer in enumerate((sib, opp, opp_sib)):
-                weight_arrival(k, peer).wait_recv()
-            wt[...] = wall[...].astype(F32).T.astype(BF16)
             cot_copy.wait()
     for r in range(done, row_blocks):
         local_products(r)
@@ -221,86 +255,37 @@
         for c in moves(way, half - 1):
             gather_arrival(way, half - 1, c).wait_recv()
 
-    def feat_move(buf, kind, hop, c, owner, peer):
-        at = buf.at[c, pl.ds(pl.multiple_of(owner * width, width), width), :]
-        return pltpu.make_async_remote_copy(
-            src_ref=at,
-            dst_ref=at,
-            send_sem=fe_send.at[kind, hop, c],
-            recv_sem=fe_recv.at[kind, hop, c],
-            device_id={"feat": peer},
-            device_id_type=MESH,
-        )
-
-    def feat_start(buf, kind, c):
-        feat_move(buf, kind, 0, c, fe, opp).start()
-        feat_move(buf, kind, 1, c, fe, sib).start()
-
-    def feat_pass(buf, kind, c):
-        feat_move(buf, kind, 0, c, opp, opp).wait_recv()
-        feat_move(buf, kind, 2, c, opp, sib).start()
-
-    def feat_arrive(buf, kind, c):
-        feat_move(buf, kind, 1, c, sib, sib).wait_recv()
-        feat_move(buf, kind, 2, c, opp_sib, sib).wait_recv()
-
-    for c in range(chunks):
-
-        def one_row(r, carry, c=c):
-            at = c * in_chunk + r
-            total = zloc[at] + products(lambda i: gbuf[cols[i]], at, TL, per_block - TL)
-            zall[c, mine, pl.ds(pl.multiple_of(r * block, block), block)] = total.astype(BF16)
-            return carry
-
-        lax.fori_loop(0, in_chunk, one_row, 0)
-        feat_start(zall, 0, c)
-        if c > 0:
-            feat_pass(zall, 0, c - 1)
-    feat_pass(zall, 0, chunks - 1)
-
-    w_cols = wt[mine, :]
-    w_rows = wall[mine, :]
     diagonal = lax.broadcasted_iota(jnp.int32, (width, width), 0) == lax.broadcasted_iota(
         jnp.int32, (width, width), 1
     )
     bias_row = jnp.broadcast_to(bias[...], (width, width))
     bias_col = jnp.sum(jnp.where(diagonal, bias_row, 0.0), axis=1, keepdims=True)
-    for c in range(chunks):
-        feat_arrive(zall, 0, c)
-        pre = jnp.dot(w_cols, zall[c], preferred_element_type=F32) + bias_col
-        sigma = jax.nn.sigmoid(pre)
-        hidden[:, c * cw : (c + 1) * cw] = (pre * sigma).astype(BF16)
-        g = cot[:, c * cw : (c + 1) * cw].astype(F32) * (sigma * (1.0 + pre * (1.0 - sigma)))
-        gall[c, mine, :] = g.astype(BF16)
-        feat_start(gall, 1, c)
-        folded = g[:, :block]
-        for b in range(1, in_chunk):
-            folded = folded + g[:, b * block : (b + 1) * block]
-        bias_acc[...] = folded if c == 0 else bias_acc[...] + folded
-        if c > 0:
-            feat_pass(gall, 1, c - 1)
-    feat_pass(gall, 1, chunks - 1)
-    hidden_out = pltpu.make_async_copy(hidden, hidden_hbm, out_sem.at[0])
-    hidden_out.start()
-
     def terms(r, first, count):
         right = jnp.concatenate([tiles[r * per_block + first + t] for t in range(count)], axis=1)
         out = jnp.dot(ubuf[r], right, preferred_element_type=F32)
         for t in range(count):
             tbuf[r * per_block + first + t] = out[:, t * block : (t + 1) * block]
 
-    w_sum = jnp.zeros((width, wall.shape[1]), F32)
     for c in range(chunks):
-        feat_arrive(gall, 1, c)
-        u = jnp.dot(w_rows, gall[c], preferred_element_type=F32).astype(BF16)
+        at = slice(c * cw, (c + 1) * cw)
+        for b in range(c * in_chunk, (c + 1) * in_chunk):
+            grad_in[:, b * block : (b + 1) * block] = zloc[b] + products(
+                lambda i: gbuf[cols[i]], b, TL, per_block - TL
+            )
+        pre = grad_in[:, at] + bias_col
+        sigma = jax.nn.sigmoid(pre)
+        hidden[:, at] = (pre * sigma).astype(BF16)
+        g = cot[:, at].astype(F32) * (sigma * (1.0 + pre * (1.0 - sigma)))
+        folded = g[:, :block]
+        for b in range(1, in_chunk):
+            folded = folded + g[:, b * block : (b + 1) * block]
+        bias_acc[...] = folded if c == 0 else bias_acc[...] + folded
         for b in range(in_chunk):
-            ubuf[c * in_chunk + b] = u[:, b * block : (b + 1) * block]
+            ubuf[c * in_chunk + b] = g[:, b * block : (b + 1) * block].astype(BF16)
             terms(c * in_chunk + b, TL, per_block - TL)
-        w_sum += lax.dot_general(
-            zall[c, mine, :], gall[c], (((1,), (1,)), ((), ())), preferred_element_type=F32
-        )
+    hidden_out = pltpu.make_async_copy(hidden, hidden_hbm, out_sem.at[0])
+    hidden_out.start()
     hid = wall.shape[1]
-    wsum[:, :hid] = w_sum
     wsum[:, hid:] = jnp.broadcast_to(jnp.sum(bias_acc[...], axis=1, keepdims=True), bias_acc.shape)
 
     piece = width // n if sum_inside else width
@@ -340,10 +325,6 @@
             device_id={"rows": owner},
             device_id_type=MESH,
         )
-
-    if sum_inside:
-        for k in range(1, n):
-            piece_copy(k).start()
 
     group = 8
     locals_count = row_blocks * TL
@@ -398,24 +379,19 @@
         list(range(chunks // 2, chunks)) + list(range(chunks // 2)),
         list(range(chunks)),
     )
+    finish = [0, 2, 1, 3] if chunks == 4 else list(range(chunks))
+    last_orders = ([2, 0, 1, 3], finish) if chunks == 4 else (finish, finish)
     done = 0
     for d in range(half, 0, -1):
         for k in range(chunks):
             for way in range(2):
-                if orders[way][k] in moves(way, d - 1):
-                    send_back(way, d, orders[way][k])
+                c = (orders if d > 1 else last_orders)[way][k]
+                if c in moves(way, d - 1):
+                    send_back(way, d, c)
             if d < half or half == 1:
                 for r in range(done, min(done + 2, row_blocks)):
                     terms(r, 0, TL)
                 done = min(done + 2, row_blocks)
-        if sum_inside and d == half - 1:
-            whole = wsum[pl.ds(pl.multiple_of(row * piece, piece), piece), :]
-            for k in range(1, n):
-                piece_copy(k).wait_recv()
-                whole = whole + wland[k]
-            wpiece[pl.ds(pl.multiple_of(row * piece, piece), piece), :] = whole * scale
-            for k in range(1, n):
-                total_copy(k).start()
     for r in range(done, row_blocks):
         terms(r, 0, TL)
     running_sums(remote_count, locals_count)
@@ -427,15 +403,47 @@
         at = pl.ds(c * cw, cw)
         return pltpu.make_async_copy(grad_in.at[:, at], grad_in_hbm.at[:, at], out_sem.at[2 + c])
 
-    for c in range(chunks):
+    def own_grad(c):
         for way in range(2):
             back_copy(way, 1, c).wait_recv()
         for b in range(c * in_chunk, (c + 1) * in_chunk):
             value = grad_in[:, b * block : (b + 1) * block]
             value = value + back[0, 0, b].astype(F32) + back[1, 0, b].astype(F32)
-            grad_in[:, b * block : (b + 1) * block] = value
+            k = b - c * in_chunk
+            gall[c, mine, k * block : (k + 1) * block] = value.astype(BF16)
+        feat_start(gall, 1, c)
+
+    def results(c, first):
+        feat_arrive(gall, 1, c)
+        term = lax.dot_general(
+            fall[c, mine, :], gall[c], (((1,), (1,)), ((), ())), preferred_element_type=F32
+        )
+        wsum[:, :hid] = term if first else wsum[:, :hid] + term
+        if sum_inside and c == finish[-1]:
+            for k in range(1, n):
+                piece_copy(k).start()
+        grad_in[:, c * cw : (c + 1) * cw] = jnp.dot(w_rows, gall[c], preferred_element_type=F32)
         grad_in_copy(c).start()
 
+    for k, c in enumerate(finish):
+        own_grad(c)
+        if k > 0:
+            feat_pass(gall, 1, finish[k - 1])
+        if k > 1:
+            results(finish[k - 2], k == 2)
+    feat_pass(gall, 1, finish[-1])
+    if chunks > 1:
+        results(finish[-2], chunks == 2)
+    results(finish[-1], chunks == 1)
+
+    if sum_inside:
+        whole = wsum[pl.ds(pl.multiple_of(row * piece, piece), piece), :]
+        for k in range(1, n):
+            piece_copy(k).wait_recv()
+            whole = whole + wland[k]
+        wpiece[pl.ds(pl.multiple_of(row * piece, piece), piece), :] = whole * scale
+        for k in range(1, n):
+            total_copy(k).start()
     if sum_inside:
         for k in range(1, n):
             total_arrival(k).wait_recv()
@@ -451,7 +459,7 @@
 
     for k, peer in enumerate((sib, opp, opp_sib)):
         weight_copy(k, peer).wait_send()
-    for kind, buf in enumerate((zall, gall)):
+    for kind, buf in enumerate((fall, gall)):
         for c in range(chunks):
             feat_move(buf, kind, 0, c, fe, opp).wait_send()
             feat_move(buf, kind, 1, c, fe, sib).wait_send()

time: 84.2 us -> 86.9 us (1.032)
  Pallas kernels: 76 us -> 78.6 us
    pallas_call x1, Pallas kernels: 76 us -> 78.6 us  [local(): pl.pallas_call(functools.partial(kernel, n, chunks, sum_inside, scale), o...]
where the time goes in v4:
time: 86.9 us; the launch traced here: 86.6 us
  Pallas kernels  78.6 us (90%)
  local copies, waits for them, and re-layouts  5.94 us (7%)
  other arithmetic  1.36 us (2%)
    pallas_call x1, Pallas kernels, local(): pl.pallas_call(functools.partial(kernel, n, chunks, sum_inside, scale), o...  78.6 us
    unnamed x12, local copies, waits for them, and re-layouts  5.94 us

profile of v4, /device:TPU:0, one launch (start us, length us, event | category | flops | bytes accessed | tf_op | source)
XLA Modules:
  0.0 86.6 jit_solution(8733619167038283161)
XLA Ops:
  0.6 0.7 fusion.2
  1.3 0.2 convert_reduce_fusion.2
  1.5 0.1 select_reduce_fusion
  1.6 0.1 slice_compare_fusion
  1.7 0.1 add_convert_fusion.keep
  1.8 0.2 convert_reduce_fusion
  2.0 0.0 copy-start
  2.0 0.9 %copy-done = bf16[64,2048]{1,0:T(8,128)(2,1)S(1)} copy-done((bf16[64,2048]{1,0:T(8,128)(2,1)S(1)}, bf16[64,2048]{1,0:T(8,128)(2,1)}, u32[]{:S(2)}) %copy-start) | copy-done | bytes 262168
  3.0 0.0 copy-start.1
  3.0 0.9 %copy-done.1 = bf16[64,2048]{1,0:T(8,128)(2,1)S(1)} copy-done((bf16[64,2048]{1,0:T(8,128)(2,1)S(1)}, bf16[64,2048]{1,0:T(8,128)(2,1)}, u32[]{:S(2)}) %copy-start.1) | copy-done | bytes 262168
  3.9 0.0 copy-start.2
  3.9 0.8 copy-done.2
  4.7 0.0 copy-start.3
  4.7 0.7 copy-done.3
  5.3 78.6 %shard_map.93 = (bf16[64,2048]{1,0:T(8,128)(2,1)S(1)}, f32[64,2048]{1,0:T(8,128)S(1)}, f32[64,256]{1,0:T(8,128)S(1)}, f32[1,64]{1,0:T(1,128)S(1)}) custom-call(s32[128]{0:T(128)S(1)} %get-tuple-element.17.cols, s32[128]{0:T(128)S(1)} %get-tuple-element.15.order, f32[128]{0:T(128)S(1)} %add_convert_fusion.keep, s32[144]{0:T(256)S(1)} %add_maximum_fusion.last, ...), custom_call_target="tpu_custom_call" | custom-call | flops 738197504 | bytes 4194304 | tf_op jit(solution)/shard_map/pallas_call | solution.py:513
  84.0 0.7 copy.14
  84.7 0.8 copy.15
  85.5 0.6 copy.16
  86.1 0.5 copy.17
  (3 shorter events, 0.0 us)
Async XLA Ops:
  2.0 1.0 %copy-start = (bf16[64,2048]{1,0:T(8,128)(2,1)S(1)}, bf16[64,2048]{1,0:T(8,128)(2,1)}, u32[]{:S(2)}) copy-start(bf16[64,2048]{1,0:T(8,128)(2,1)} %feats.1) | copy-start | bytes 786436
  3.0 0.9 %copy-start.1 = (bf16[64,2048]{1,0:T(8,128)(2,1)S(1)}, bf16[64,2048]{1,0:T(8,128)(2,1)}, u32[]{:S(2)}) copy-start(bf16[64,2048]{1,0:T(8,128)(2,1)} %cot_hbm.1) | copy-start | bytes 786436
  3.9 0.8 copy-start.2
  4.7 0.7 copy-start.3

commit v5 on v2

--- a/solution.py
+++ b/solution.py
@@ -75,6 +75,7 @@
     in_chunk = row_blocks // chunks
     cw = in_chunk * block
     half = n // 2
+    ahead = 1 if chunks == 8 else 2
     row = lax.axis_index("rows")
     fe = lax.axis_index("feat")
     odd = lax.rem(row, 2)
@@ -207,9 +208,9 @@
             if d == 1 and c == 0:
                 tile_copy.wait()
             if done < row_blocks:
-                for r in range(done, min(done + 2, row_blocks)):
+                for r in range(done, min(done + ahead, row_blocks)):
                     local_products(r)
-                done = min(done + 2, row_blocks)
+                done = min(done + ahead, row_blocks)
         if d == 1:
             for k, peer in enumerate((sib, opp, opp_sib)):
                 weight_arrival(k, peer).wait_recv()
@@ -405,9 +406,9 @@
                 if orders[way][k] in moves(way, d - 1):
                     send_back(way, d, orders[way][k])
             if d < half or half == 1:
-                for r in range(done, min(done + 2, row_blocks)):
+                for r in range(done, min(done + ahead, row_blocks)):
                     terms(r, 0, TL)
-                done = min(done + 2, row_blocks)
+                done = min(done + ahead, row_blocks)
         if sum_inside and d == half - 1:
             whole = wsum[pl.ds(pl.multiple_of(row * piece, piece), piece), :]
             for k in range(1, n):
@@ -473,7 +474,7 @@
     n = lax.axis_size("rows")
     row_blocks = nodes // block
     per_block = count // row_blocks
-    chunks = 4 if n <= 8 else 2
+    chunks = 8 if n <= 8 else 2
     half = n // 2
     sum_inside = n == 8
     scale = 1.0 / math.sqrt(nodes * n)

time: 84.2 us -> 94.5 us (1.12)
  Pallas kernels: 76 us -> 86.3 us
    pallas_call x1, Pallas kernels: 76 us -> 86.3 us  [local(): pl.pallas_call(functools.partial(kernel, n, chunks, sum_inside, scale), o...]
where the time goes in v5:
time: 94.5 us; the launch traced here: 94.3 us
  Pallas kernels  86.3 us (91%)
  local copies, waits for them, and re-layouts  5.94 us (6%)
  other arithmetic  1.36 us (1%)
    pallas_call x1, Pallas kernels, local(): pl.pallas_call(functools.partial(kernel, n, chunks, sum_inside, scale), o...  86.3 us
    unnamed x12, local copies, waits for them, and re-layouts  5.94 us

profile of v5, /device:TPU:0, one launch (start us, length us, event | category | flops | bytes accessed | tf_op | source)
XLA Modules:
  0.0 94.3 jit_solution(17276779440777214063)
XLA Ops:
  0.6 0.7 fusion.2
  1.3 0.2 convert_reduce_fusion.2
  1.5 0.1 select_reduce_fusion
  1.6 0.1 slice_compare_fusion
  1.7 0.1 add_convert_fusion.keep
  1.8 0.2 convert_reduce_fusion
  2.0 0.0 copy-start
  2.0 0.9 copy-done
  3.0 0.0 copy-start.1
  3.0 0.9 %copy-done.1 = bf16[64,2048]{1,0:T(8,128)(2,1)S(1)} copy-done((bf16[64,2048]{1,0:T(8,128)(2,1)S(1)}, bf16[64,2048]{1,0:T(8,128)(2,1)}, u32[]{:S(2)}) %copy-start.1) | copy-done | bytes 262168
  3.9 0.0 copy-start.2
  3.9 0.8 copy-done.2
  4.7 0.0 copy-start.3
  4.7 0.7 copy-done.3
  5.3 86.3 %shard_map.93 = (bf16[64,2048]{1,0:T(8,128)(2,1)S(1)}, f32[64,2048]{1,0:T(8,128)S(1)}, f32[64,256]{1,0:T(8,128)S(1)}, f32[1,64]{1,0:T(1,128)S(1)}) custom-call(s32[128]{0:T(128)S(1)} %get-tuple-element.17.cols, s32[128]{0:T(128)S(1)} %get-tuple-element.15.order, f32[128]{0:T(128)S(1)} %add_convert_fusion.keep, s32[144]{0:T(256)S(1)} %add_maximum_fusion.last, ...), custom_call_target="tpu_custom_call" | custom-call | flops 738197504 | bytes 4194304 | tf_op jit(solution)/shard_map/pallas_call | solution.py:506
  91.6 0.7 copy.14
  92.3 0.8 copy.15
  93.1 0.6 copy.16
  93.8 0.5 copy.17
  (3 shorter events, 0.0 us)
Async XLA Ops:
  2.0 1.0 %copy-start = (bf16[64,2048]{1,0:T(8,128)(2,1)S(1)}, bf16[64,2048]{1,0:T(8,128)(2,1)}, u32[]{:S(2)}) copy-start(bf16[64,2048]{1,0:T(8,128)(2,1)} %feats.1) | copy-start | bytes 786436
  3.0 0.9 %copy-start.1 = (bf16[64,2048]{1,0:T(8,128)(2,1)S(1)}, bf16[64,2048]{1,0:T(8,128)(2,1)}, u32[]{:S(2)}) copy-start(bf16[64,2048]{1,0:T(8,128)(2,1)} %cot_hbm.1) | copy-start | bytes 786436
  3.9 0.8 copy-start.2
  4.7 0.7 copy-start.3

commit v6 on v2

--- a/solution.py
+++ b/solution.py
@@ -207,9 +207,9 @@
             if d == 1 and c == 0:
                 tile_copy.wait()
             if done < row_blocks:
-                for r in range(done, min(done + 2, row_blocks)):
+                for r in range(done, min(done + 4, row_blocks)):
                     local_products(r)
-                done = min(done + 2, row_blocks)
+                done = min(done + 4, row_blocks)
         if d == 1:
             for k, peer in enumerate((sib, opp, opp_sib)):
                 weight_arrival(k, peer).wait_recv()
@@ -405,9 +405,9 @@
                 if orders[way][k] in moves(way, d - 1):
                     send_back(way, d, orders[way][k])
             if d < half or half == 1:
-                for r in range(done, min(done + 2, row_blocks)):
+                for r in range(done, min(done + 4, row_blocks)):
                     terms(r, 0, TL)
-                done = min(done + 2, row_blocks)
+                done = min(done + 4, row_blocks)
         if sum_inside and d == half - 1:
             whole = wsum[pl.ds(pl.multiple_of(row * piece, piece), piece), :]
             for k in range(1, n):
@@ -473,7 +473,7 @@
     n = lax.axis_size("rows")
     row_blocks = nodes // block
     per_block = count // row_blocks
-    chunks = 4 if n <= 8 else 2
+    chunks = 2
     half = n // 2
     sum_inside = n == 8
     scale = 1.0 / math.sqrt(nodes * n)

time: 84.2 us -> 81.1 us (0.963)
  Pallas kernels: 76 us -> 72.8 us
    pallas_call x1, Pallas kernels: 76 us -> 72.8 us  [local(): pl.pallas_call(functools.partial(kernel, n, chunks, sum_inside, scale), o...]
where the time goes in v6:
time: 81.1 us; the launch traced here: 80.8 us
  Pallas kernels  72.8 us (90%)
  local copies, waits for them, and re-layouts  5.94 us (7%)
  other arithmetic  1.36 us (2%)
    pallas_call x1, Pallas kernels, local(): pl.pallas_call(functools.partial(kernel, n, chunks, sum_inside, scale), o...  72.8 us
    unnamed x12, local copies, waits for them, and re-layouts  5.94 us

profile of v6, /device:TPU:0, one launch (start us, length us, event | category | flops | bytes accessed | tf_op | source)
XLA Modules:
  0.0 80.8 jit_solution(8599430138809419736)
XLA Ops:
  0.6 0.7 fusion.2
  1.3 0.2 convert_reduce_fusion.2
  1.5 0.1 select_reduce_fusion
  1.6 0.1 slice_compare_fusion
  1.7 0.1 add_convert_fusion.keep
  1.8 0.2 convert_reduce_fusion
  2.0 0.0 copy-start
  2.0 0.9 %copy-done = bf16[64,2048]{1,0:T(8,128)(2,1)S(1)} copy-done((bf16[64,2048]{1,0:T(8,128)(2,1)S(1)}, bf16[64,2048]{1,0:T(8,128)(2,1)}, u32[]{:S(2)}) %copy-start) | copy-done | bytes 262168
  3.0 0.0 copy-start.1
  3.0 0.9 %copy-done.1 = bf16[64,2048]{1,0:T(8,128)(2,1)S(1)} copy-done((bf16[64,2048]{1,0:T(8,128)(2,1)S(1)}, bf16[64,2048]{1,0:T(8,128)(2,1)}, u32[]{:S(2)}) %copy-start.1) | copy-done | bytes 262168
  3.9 0.0 copy-start.2
  3.9 0.8 copy-done.2
  4.7 0.0 copy-start.3
  4.7 0.7 copy-done.3
  5.3 72.8 %shard_map.93 = (bf16[64,2048]{1,0:T(8,128)(2,1)S(1)}, f32[64,2048]{1,0:T(8,128)S(1)}, f32[64,256]{1,0:T(8,128)S(1)}, f32[1,64]{1,0:T(1,128)S(1)}) custom-call(s32[128]{0:T(128)S(1)} %get-tuple-element.17.cols, s32[128]{0:T(128)S(1)} %get-tuple-element.15.order, f32[128]{0:T(128)S(1)} %add_convert_fusion.keep, s32[144]{0:T(256)S(1)} %add_maximum_fusion.last, ...), custom_call_target="tpu_custom_call" | custom-call | flops 738197504 | bytes 4194304 | tf_op jit(solution)/shard_map/pallas_call | solution.py:505
  78.2 0.7 copy.14
  78.9 0.8 copy.15
  79.7 0.6 copy.16
  80.3 0.5 copy.17
  (3 shorter events, 0.0 us)
Async XLA Ops:
  2.0 1.0 %copy-start = (bf16[64,2048]{1,0:T(8,128)(2,1)S(1)}, bf16[64,2048]{1,0:T(8,128)(2,1)}, u32[]{:S(2)}) copy-start(bf16[64,2048]{1,0:T(8,128)(2,1)} %feats.1) | copy-start | bytes 786436
  3.0 0.9 %copy-start.1 = (bf16[64,2048]{1,0:T(8,128)(2,1)S(1)}, bf16[64,2048]{1,0:T(8,128)(2,1)}, u32[]{:S(2)}) copy-start(bf16[64,2048]{1,0:T(8,128)(2,1)} %cot_hbm.1) | copy-start | bytes 786436
  3.9 0.8 copy-start.2
  4.7 0.7 copy-start.3
